TPU v7x, 512 devices: a whole 4x8x8 slice. The times are simulated.
512 devices in a mesh: rep: 8 (over z_hi, x), fsdp: 64 (over y, z_lo, core).
Axes of the slice: x: 4, y: 8, z: 8 (z_hi: 2, z_lo: 4; z = z_hi * 4 + z_lo), core: 2. Of those that a mesh axis runs over, the one named last changes fastest.
Arguments:
- activations: bfloat16 [8, 8192, 8192], P('rep', 'fsdp'), may hold values from -6 to 6
- cotangent: bfloat16 [8, 8192, 512], P('rep', 'fsdp'), may hold values from -6 to 6
- local_weight: bfloat16 [8, 8192, 512], P('rep', 'fsdp'), may hold values from -6 to 6
- norm_gain: float32 [8, 8192], P('rep', 'fsdp'), may hold values from 0.5 to 1.5
- global_weight: float32 [8192, 512], P('fsdp'), may hold values from -6 to 6
- momentum: float32 [8192, 512], P('fsdp'), may hold values from -4 to 4
- codes: bfloat16 [8, 8192, 512], P('rep', 'fsdp'), may hold values from -30 to 30, as said below
- exponents: int32 [8, 8192, 4], P('rep', 'fsdp'), may hold values from -7 to -3
Outputs:
- new_local: float32 [8, 8192, 512], P('rep', 'fsdp')
- new_gain: float32 [8, 8192], P('rep', 'fsdp')
- new_global: float32 [8192, 512], P('fsdp')
- new_momentum: float32 [8192, 512], P('fsdp')
Inputs may be any that keep to these rules, and one draw needn't show every extreme that they name: `codes`: every entry is s (1 + m / 8) 2 ** k with s = 1 or -1, m in 0..7 and k in -3..4, a value of an 8-bit float with four exponent and three mantissa bits.
All inputs are finite; a program needn't handle non-finite values.
Results may differ from a plain program's by a relative error of at most 0.00038.
Values may be sent and summed in bfloat16 or wider, within the bound.
A program may use at most 64 MiB of HBM per device.

v0:
```python
import math

import jax
import jax.numpy as jnp
from jax import lax
from jax.sharding import PartitionSpec as P


def outer_sync(global_weight, momentum, codes, exponents):
    replicas = lax.axis_size("rep")
    rows, width = global_weight.shape
    blocks = exponents.shape[2]
    scales = jnp.exp2(exponents.astype(jnp.float32))
    decoded = (
        codes[0].astype(jnp.float32).reshape(rows, blocks, width // blocks) * scales[0][..., None]
    )
    total = lax.psum(decoded.reshape(rows, width), "rep")
    average = total / replicas
    new_momentum = 0.9 * momentum + average
    new_global = global_weight - 0.7 * (average + 0.9 * new_momentum)
    return (new_global, new_momentum)


def inner_backward(activations, cotangent, local_weight, norm_gain):
    width = activations.shape[2]
    values = activations[0].astype(jnp.float32)
    normed = (values * lax.rsqrt(jnp.mean(values * values, axis=-1, keepdims=True) + 1e-05)).astype(
        jnp.bfloat16
    )
    normed_cols = lax.all_to_all(normed, "fsdp", split_axis=1, concat_axis=0, tiled=True)
    weight_half = local_weight[0]
    piece = lax.all_gather(cotangent[0], "fsdp", axis=0, tiled=True)
    grad_part = lax.dot_general(
        normed_cols, piece, (((0,), (0,)), ((), ())), preferred_element_type=jnp.float32
    )
    back_part = lax.dot_general(
        piece, weight_half, (((1,), (1,)), ((), ())), preferred_element_type=jnp.float32
    ) / math.sqrt(width)
    gain_part = jnp.sum(back_part * normed_cols.astype(jnp.float32), axis=0)
    weight_grad = norm_gain[0][:, None] * grad_part / math.sqrt(width)
    stepped = weight_half.astype(jnp.float32) - 0.2 * weight_grad
    new_gain = norm_gain[0] - 0.005 * gain_part
    return (stepped, new_gain)


def shards(
    activations, cotangent, local_weight, norm_gain, global_weight, momentum, codes, exponents
):
    stepped, new_gain = inner_backward(activations, cotangent, local_weight, norm_gain)
    new_global, new_momentum = outer_sync(global_weight, momentum, codes, exponents)
    new_local = 0.5 * stepped + 0.5 * new_global
    return (new_local[None], new_gain[None], new_global, new_momentum)


def solution(mesh):
    placed = (
        P("rep", "fsdp", None),
        P("rep", "fsdp", None),
        P("rep", "fsdp", None),
        P("rep", "fsdp"),
        P("fsdp", None),
        P("fsdp", None),
        P("rep", "fsdp", None),
        P("rep", "fsdp", None),
    )
    return jax.shard_map(
        shards,
        mesh=mesh,
        in_specs=placed,
        out_specs=(P("rep", "fsdp", None), P("rep", "fsdp"), P("fsdp", None), P("fsdp", None)),
        check_vma=False,
    )
```

profile of v0, /device:TPU:1, one launch (start us, length us, event | category | flops | bytes accessed | tf_op | source)
XLA Modules:
  0.0 199.2 jit_solution(1115046380763724440)
XLA Ops:
  8.0 0.0 all-reduce.2.cloned.1.call-start
  8.0 0.7 exponential_bitcast_fusion
  8.7 0.1 copy.13
  8.8 0.2 mul.86
  9.0 1.6 bitcast_multiply_fusion
  10.7 0.0 all-reduce.2.cloned.1.call-update
  10.7 0.0 all-gather.3.cloned.1.call-start
  10.8 0.5 all-gather.3.cloned.1.call-update
  11.3 2.0 %convert_bitcast_fusion = f32[16,8,64,128]{3,1,2,0:T(8,128)S(1)} fusion(bf16[1,128,8192]{2,1,0:T(8,128)(2,1)} %param.8), kind=kLoop, calls=%fused_computation.6 | loop fusion | flops 1048576 | bytes 6291456
  13.3 0.0 copy-start.1
  13.3 0.7 copy.14
  14.1 0.8 copy-done.1
  14.9 0.5 fusion.4
  15.4 0.0 copy-start.3
  15.4 0.0 copy-start.4
  15.4 3.8 %fusion.5 = bf16[128,64,128]{2,0,1:T(8,128)(2,1)} fusion(f32[128,64,128]{2,1,0:T(8,128)S(1)} %bitcast.44, f32[128]{0:T(128)S(1)} %add_rsqrt_fusion), kind=kLoop, calls=%fused_computation.9 | loop fusion | flops 2097152 | bytes 6291968 | tf_op jit(solution)/shard_map/convert_element_type | solution.py:27
  19.2 0.0 copy-start.5
  19.2 14.7 %all-to-all-start = ((bf16[128,64,128]{2,0,1:T(8,128)(2,1)}), bf16[128,64,128]{2,0,1:T(8,128)(2,1)S(1)}, u32[]{:S(2)}, u32[]{:S(2)}) async-start(bf16[128,64,128]{2,0,1:T(8,128)(2,1)} %fusion.5), calls=%async_computation | async-start | bytes 4194304 | tf_op jit(solution)/shard_map/all_to_all | solution.py:30
  33.9 114.5 %all-reduce.2.cloned.1.call-done = f32[128,512]{1,0:T(8,128)} async-done(((f32[128,512]{1,0:T(8,128)}), f32[128,512]{1,0:T(8,128)}) %all-reduce.2.cloned.1.call-update) | async-done | bytes 262160 | tf_op jit(solution)/shard_map/psum | solution.py:17
  148.4 0.0 copy-done.3
  148.4 0.0 copy-done.4
  148.4 1.7 multiply_subtract_fusion
  150.1 0.0 copy-start.2
  150.1 0.0 all-to-all-done
  150.1 33.2 %all-gather.3.cloned.1.call-done = bf16[1,8192,512]{2,1,0:T(8,128)(2,1)} async-done(((bf16[1,128,512]{2,1,0:T(8,128)(2,1)}), bf16[1,8192,512]{2,1,0:T(8,128)(2,1)}) %all-gather.3.cloned.1.call-update) | async-done | bytes 8388624 | tf_op jit(solution)/shard_map/all_gather | solution.py:32
  183.4 0.0 copy-done.5
  183.4 0.0 copy-start.6
  183.4 0.0 copy-start
  183.4 5.9 %fusion.6 = f32[128]{0:T(128)S(1)} fusion(bf16[8192,128]{1,0:T(8,128)(2,1)S(1)} %bitcast.45, bf16[1,8192,512]{2,1,0:T(8,128)(2,1)} %all-gather.3.cloned.1.call-done, bf16[1,128,512]{2,1,0:T(8,128)(2,1)S(1)} %copy-done.5), kind=kOutput, calls=%fused_computation.10 | convolution fusion | flops 1077936000 | bytes 10617344 | tf_op jit(solution)/shard_map/dot_general | solution.py:36
  189.3 0.0 copy-done.6
  189.3 0.5 bitcast_subtract_fusion
  189.8 0.0 copy-done.2
  189.8 0.0 copy-done
  189.8 2.0 %fusion.24 = f32[1,128,512]{2,1,0:T(8,128)} fusion(f32[128,512]{1,0:T(8,128)S(1)} %get-tuple-element.4, bf16[8192,128]{1,0:T(8,128)(2,1)S(1)} %bitcast.46, bf16[1,8192,512]{2,1,0:T(8,128)(2,1)S(1)} %copy-done, bf16[1,128,512]{2,1,0:T(8,128)(2,1)S(1)} %copy-done.5, f32[128]{0:T(128)S(1)} %bitcast.48), kind=kOutput, calls=%fused_computation.16 | convolution fusion | flops 1074135040 | bytes 11141632 | tf_op jit(solution)/shard_map/dot_general | solution.py:33
  (1 shorter events, 0.0 us)
Async XLA Ops:
  8.0 140.4 %all-reduce.2.cloned.1.call-start = ((), (), s32[]{:S(2)}) async-start(), calls=%async_computation.1 | async-start | bytes 524288 | tf_op jit(solution)/shard_map/psum | solution.py:17
  10.7 172.6 %all-gather.3.cloned.1.call-start = ((), (), s32[]{:S(2)}) async-start(), calls=%async_computation.2 | async-start | bytes 8519680 | tf_op jit(solution)/shard_map/all_gather | solution.py:32
  13.3 1.6 copy-start.1
  15.4 133.0 %copy-start.3 = (f32[128,512]{1,0:T(8,128)S(1)}, f32[128,512]{1,0:T(8,128)}, u32[]{:S(2)}) copy-start(f32[128,512]{1,0:T(8,128)} %param.12) | copy-start | bytes 786436
  15.4 133.0 %copy-start.4 = (f32[128,512]{1,0:T(8,128)S(1)}, f32[128,512]{1,0:T(8,128)}, u32[]{:S(2)}) copy-start(f32[128,512]{1,0:T(8,128)} %param.13) | copy-start | bytes 786436
  19.2 164.1 %copy-start.5 = (bf16[1,128,512]{2,1,0:T(8,128)(2,1)S(1)}, bf16[1,128,512]{2,1,0:T(8,128)(2,1)}, u32[]{:S(2)}) copy-start(bf16[1,128,512]{2,1,0:T(8,128)(2,1)} %param.10) | copy-start | bytes 393220
  19.2 130.9 %all-to-all-start = ((bf16[128,64,128]{2,0,1:T(8,128)(2,1)}), bf16[128,64,128]{2,0,1:T(8,128)(2,1)S(1)}, u32[]{:S(2)}, u32[]{:S(2)}) async-start(bf16[128,64,128]{2,0,1:T(8,128)(2,1)} %fusion.5), calls=%async_computation | async-start | bytes 4194304 | tf_op jit(solution)/shard_map/all_to_all | solution.py:30
  150.1 39.6 %copy-start.2 = (f32[128,512]{1,0:T(8,128)}, f32[128,512]{1,0:T(8,128)S(1)}, u32[]{:S(2)}) copy-start(f32[128,512]{1,0:T(8,128)S(1)} %get-tuple-element.4) | copy-start | bytes 786436
  183.4 5.9 %copy-start.6 = (f32[1,128]{1,0:T(1,128)S(1)}, f32[1,128]{1,0:T(1,128)}, u32[]{:S(2)}) copy-start(f32[1,128]{1,0:T(1,128)} %param.11) | copy-start | bytes 1540
  183.4 6.4 %copy-start = (bf16[1,8192,512]{2,1,0:T(8,128)(2,1)S(1)}, bf16[1,8192,512]{2,1,0:T(8,128)(2,1)}, u32[]{:S(2)}) copy-start(bf16[1,8192,512]{2,1,0:T(8,128)(2,1)} %all-gather.3.cloned.1.call-done) | copy-start | bytes 25165828
Sparse Core Ops, SparseCore 0:
  12.3 136.0 all-reduce.1
Sparse Core Ops, SparseCore 1:
  13.6 169.7 all-gather.2
where the time goes:
time: 200 us; the launch traced here: 199 us
  waiting for transfers between devices  148 us (74%)
  between operations  15.5 us (8%)
  starting transfers between devices  14.8 us (7%)
  other arithmetic  10.9 us (5%)
  matrix products  7.91 us (4%)
    psum x1, waiting for transfers between devices, outer_sync(): total = lax.psum(decoded.reshape(rows, width), 'rep')  114 us
    all_gather x1, waiting for transfers between devices, inner_backward(): piece = lax.all_gather(cotangent[0], 'fsdp', axis=0, tiled=True)  33.2 us
    all_to_all x1, starting transfers between devices, inner_backward(): lax.all_to_all(normed, 'fsdp', split_axis=1, concat_axis=0, tiled=True)  14.7 us
    dot_general x1, matrix products, inner_backward(): lax.dot_general(piece, weight_half, (((1,), (1,)), ((), ())), preferred_e...  5.89 us
  transfers between devices with their start and end apart: 3, of which 2 were waited for; matrix products, arithmetic and copies ran while one was open for 4% of the time, Pallas kernels for 0%

commit v1 on v0

v1 whole, which is shorter than its diff:
```python
import functools
import math

import jax
import jax.numpy as jnp
from jax import lax
from jax.experimental import pallas as pl
from jax.experimental.pallas import tpu as pltpu
from jax.sharding import PartitionSpec as P

MESH = pl.DeviceIdType.MESH
YS, ZS, XS = 8, 4, 4
F32, BF16 = jnp.float32, jnp.bfloat16


def flip(value, mask):
    low, high = lax.rem(value, 2), value // 2
    if mask & 1:
        low = 1 - low
    if mask & 2:
        high = 1 - high
    return high * 2 + low


def column(row, eye):
    return jnp.sum(jnp.where(eye, row, 0.0), axis=1, keepdims=True)


def product(lhs, rhs):
    return lax.dot_general(lhs, rhs, (((0,), (0,)), ((), ())), preferred_element_type=F32)


def kernel(
    act_hbm, cot_hbm, weight_hbm, gain_hbm, global_hbm, momentum_hbm, codes_hbm, exps_hbm,
    local_out, gain_out, global_out, momentum_out,
    act, normed, recv, cots, weight, gain, outer, mom, codes, exps,
    part_sib, part_own, from_sib, from_z, decoded, x_in, x_sum, h_in, total,
    in_sem, cot_s, cot_r, a2a_s, a2a_r, sib_s, sib_r, z_s, z_r, x1_s, x1_r, h_s, h_r, x2_s, x2_r,
):
    rep, pos = lax.axis_index("rep"), lax.axis_index("fsdp")
    zh, x = rep // XS, lax.rem(rep, XS)
    y, z, core = pos // (2 * ZS), lax.rem(pos // 2, ZS), lax.rem(pos, 2)
    width = act.shape[1]

    def at(yy=None, zz=None, cc=None, xx=None, hh=None):
        yy = y if yy is None else yy
        zz = z if zz is None else zz
        cc = core if cc is None else cc
        xx = x if xx is None else xx
        hh = zh if hh is None else hh
        return (hh * XS + xx, (yy * ZS + zz) * 2 + cc)

    def y_off(d):
        return at(yy=lax.rem(y + d, YS))

    def x_off(d):
        return at(xx=lax.rem(x + d, XS))

    def send(src, dst, ssem, rsem, device):
        return pltpu.make_async_remote_copy(
            src_ref=src, dst_ref=dst, send_sem=ssem, recv_sem=rsem, device_id=device, device_id_type=MESH
        )

    sibling = at(cc=1 - core)
    other = at(hh=1 - zh)

    loads = [
        pltpu.make_async_copy(cot_hbm.at[0], cots.at[0], in_sem.at[0]),
        pltpu.make_async_copy(codes_hbm.at[0], codes, in_sem.at[1]),
        pltpu.make_async_copy(exps_hbm, exps, in_sem.at[2]),
        pltpu.make_async_copy(act_hbm.at[0], act, in_sem.at[3]),
        pltpu.make_async_copy(weight_hbm.at[0], weight, in_sem.at[4]),
        pltpu.make_async_copy(gain_hbm, gain, in_sem.at[5]),
        pltpu.make_async_copy(global_hbm, outer, in_sem.at[6]),
        pltpu.make_async_copy(momentum_hbm, mom, in_sem.at[7]),
    ]
    for load in loads:
        load.start()

    barrier = pltpu.get_barrier_semaphore()
    peers = [y_off(d) for d in range(1, YS)] + [at(zz=flip(z, q)) for q in (1, 2, 3)]
    peers += [sibling, other] + [x_off(d) for d in range(1, XS)]
    for peer in peers:
        pl.semaphore_signal(barrier, inc=1, device_id=peer, device_id_type=MESH)

    eye = lax.broadcasted_iota(jnp.int32, (128, 128), 0) == lax.broadcasted_iota(
        jnp.int32, (128, 128), 1
    )
    loads[1].wait()
    loads[2].wait()
    scales = jnp.exp2(exps[...].astype(F32))
    for b in range(4):
        cols = slice(b * 128, (b + 1) * 128)
        scale = column(scales[b : b + 1, :], eye)
        decoded[:, cols] = (codes[:, cols].astype(F32) * scale).astype(BF16)

    pl.semaphore_wait(barrier, len(peers))

    up, down = y_off(1), y_off(YS - 1)
    loads[0].wait()
    hops_up = [send(cots.at[i], cots.at[i + 1], cot_s.at[i], cot_r.at[i], up) for i in range(3)]
    hops_up.append(send(cots.at[3, 0:64], cots.at[4, 0:64], cot_s.at[3], cot_r.at[3], up))
    hops_down = [
        send(cots.at[(8 - i) % 8], cots.at[7 - i], cot_s.at[4 + i], cot_r.at[4 + i], down)
        for i in range(3)
    ]
    hops_down.append(send(cots.at[5, 64:128], cots.at[4, 64:128], cot_s.at[7], cot_r.at[7], down))
    hops_up[0].start()
    hops_down[0].start()

    x_parts = []
    for d in range(1, XS):
        rows = pl.ds(pl.multiple_of(lax.rem(x + d, XS) * 32, 32), 32)
        x_parts.append(send(decoded.at[rows], x_in.at[d - 1], x1_s.at[d - 1], x1_r.at[d - 1], x_off(d)))
    for part in x_parts:
        part.start()

    loads[3].wait()

    @pl.loop(0, 8)
    def _(group):
        rows = pl.ds(pl.multiple_of(group * 16, 16), 16)
        squares = jnp.zeros((16, 256), F32)
        for b in range(32):
            values = act[rows, b * 256 : (b + 1) * 256].astype(F32)
            squares += values * values
        mean = jnp.sum(squares, axis=1, keepdims=True) / width
        scale = lax.rsqrt(mean + 1e-05)
        for b in range(32):
            values = act[rows, b * 256 : (b + 1) * 256].astype(F32)
            normed[b, rows, :] = (values * scale).astype(BF16)

    def push(k):
        zz = flip(z, 3 - k)
        for d in range(1, YS):
            yy = lax.rem(y + d, YS)
            send(normed.at[yy * ZS + zz], recv.at[k, d], a2a_s.at[k], a2a_r.at[k], at(yy=yy)).start()
        recv[k, 0] = normed[y * ZS + zz]

    def multiply(k):
        seven = pltpu.make_async_copy(recv.at[k, 1:8], recv.at[k, 1:8], a2a_r.at[k])
        seven.wait()
        rhs = cots[...].reshape(1024, 512)

        def part(c):
            cols = pl.ds(pl.multiple_of(c * 128, 128), 128)
            return product(recv[k, :, :, cols].reshape(1024, 128), rhs)

        part_sib[k] = part(1 - core)
        send(part_sib.at[k], from_sib.at[k], sib_s.at[k], sib_r.at[k], sibling).start()
        part_own[k] = part(core)

    def sib_copy(k):
        return send(part_sib.at[k], from_sib.at[k], sib_s.at[k], sib_r.at[k], sibling)

    def z_copy(k):
        return send(part_own.at[k], from_z.at[k], z_s.at[k], z_r.at[k], at(zz=flip(z, 3 - k)))

    def scatter(k):
        sib_copy(k).wait_recv()
        part_own[k] = part_own[k] + from_sib[k]
        z_copy(k).start()

    push(0)
    hops_up[0].wait_recv()
    hops_down[0].wait_recv()
    hops_up[1].start()
    hops_down[1].start()
    push(1)

    for part in x_parts:
        part.wait_recv()
    mine = pl.ds(pl.multiple_of(x * 32, 32), 32)
    x_sum[...] = (
        decoded[mine, :].astype(F32) + x_in[0].astype(F32) + x_in[1].astype(F32) + x_in[2].astype(F32)
    )
    h_copy = send(x_sum, h_in, h_s.at[0], h_r.at[0], other)
    h_copy.start()

    hops_up[1].wait_recv()
    hops_down[1].wait_recv()
    hops_up[2].start()
    hops_down[2].start()

    h_copy.wait_recv()
    total[mine, :] = x_sum[...] + h_in[...]
    totals = [
        send(total.at[mine], total.at[mine], x2_s.at[d - 1], x2_r.at[d - 1], x_off(d))
        for d in range(1, XS)
    ]
    for copy in totals:
        copy.start()

    hops_up[2].wait_recv()
    hops_down[2].wait_recv()
    hops_up[3].start()
    hops_down[3].start()
    push(2)
    hops_up[3].wait_recv()
    hops_down[3].wait_recv()

    multiply(0)
    push(3)
    scatter(0)
    multiply(1)
    scatter(1)

    for copy in totals:
        copy.wait_recv()
    for load in loads[4:]:
        load.wait()
    average = total[...] / 8.0
    momentum = 0.9 * mom[...] + average
    momentum_out[...] = momentum
    outer_new = outer[...] - 0.7 * (average + 0.9 * momentum)
    global_out[...] = outer_new

    multiply(2)
    scatter(2)
    multiply(3)
    for k in range(3):
        z_copy(k).wait_recv()
    sib_copy(3).wait_recv()
    summed = part_own[3] + from_sib[3] + from_z[0] + from_z[1] + from_z[2]

    root = math.sqrt(width)
    held = weight[...].astype(F32)
    gain_grad = jnp.sum(held * summed, axis=1, keepdims=True) / root
    gain_row = jnp.sum(jnp.where(eye, gain_grad, 0.0), axis=0, keepdims=True)
    gain_out[...] = gain[...] - 0.005 * gain_row
    weight_grad = column(gain[...], eye) * summed / root
    local_out[0] = 0.5 * (held - 0.2 * weight_grad) + 0.5 * global_out[...]

    for copy in hops_up + hops_down + x_parts + [h_copy] + totals:
        copy.wait_send()
    for k in range(4):
        pltpu.make_async_copy(normed.at[0:7], normed.at[0:7], a2a_s.at[k]).wait()
        sib_copy(k).wait_send()
    for k in range(3):
        z_copy(k).wait_send()


def shards(
    activations, cotangent, local_weight, norm_gain, global_weight, momentum, codes, exponents
):
    rows, width = global_weight.shape
    any_spec = pl.BlockSpec(memory_space=pl.ANY)
    vmem_spec = pl.BlockSpec(memory_space=pltpu.VMEM)
    sem = pltpu.SemaphoreType.DMA
    out_shape = (
        jax.ShapeDtypeStruct((1, rows, width), F32),
        jax.ShapeDtypeStruct((1, rows), F32),
        jax.ShapeDtypeStruct((rows, width), F32),
        jax.ShapeDtypeStruct((rows, width), F32),
    )
    return pl.pallas_call(
        kernel,
        out_shape=out_shape,
        in_specs=[any_spec] * 8,
        out_specs=(vmem_spec,) * 4,
        scratch_shapes=[
            pltpu.VMEM((128, 8192), BF16),
            pltpu.VMEM((32, 128, 256), BF16),
            pltpu.VMEM((4, 8, 128, 256), BF16),
            pltpu.VMEM((8, 128, 512), BF16),
            pltpu.VMEM((128, 512), BF16),
            pltpu.VMEM((1, 128), F32),
            pltpu.VMEM((128, 512), F32),
            pltpu.VMEM((128, 512), F32),
            pltpu.VMEM((128, 512), BF16),
            pltpu.VMEM((4, 128), jnp.int32),
            pltpu.VMEM((4, 128, 512), F32),
            pltpu.VMEM((4, 128, 512), F32),
            pltpu.VMEM((4, 128, 512), F32),
            pltpu.VMEM((3, 128, 512), F32),
            pltpu.VMEM((128, 512), BF16),
            pltpu.VMEM((3, 32, 512), BF16),
            pltpu.VMEM((32, 512), F32),
            pltpu.VMEM((32, 512), F32),
            pltpu.VMEM((128, 512), F32),
            sem((8,)),
            sem((8,)),
            sem((8,)),
            sem((4,)),
            sem((4,)),
            sem((4,)),
            sem((4,)),
            sem((3,)),
            sem((3,)),
            sem((3,)),
            sem((3,)),
            sem((1,)),
            sem((1,)),
            sem((3,)),
            sem((3,)),
        ],
        compiler_params=pltpu.CompilerParams(
            collective_id=0, has_side_effects=True, vmem_limit_bytes=40 << 20
        ),
        name="sync_and_step",
    )(
        activations, cotangent, local_weight, norm_gain, global_weight, momentum, codes,
        jnp.transpose(exponents[0]),
    )


def solution(mesh):
    placed = (
        P("rep", "fsdp", None),
        P("rep", "fsdp", None),
        P("rep", "fsdp", None),
        P("rep", "fsdp"),
        P("fsdp", None),
        P("fsdp", None),
        P("rep", "fsdp", None),
        P("rep", "fsdp", None),
    )
    return jax.shard_map(
        shards,
        mesh=mesh,
        in_specs=placed,
        out_specs=(P("rep", "fsdp", None), P("rep", "fsdp"), P("fsdp", None), P("fsdp", None)),
        check_vma=False,
    )
```

time: 200 us -> 91.1 us (0.46)
  waiting for transfers between devices: 148 us -> 0 us
  Pallas kernels: 0 us -> 80 us
  between operations: 15.5 us -> 0.66 us
  starting transfers between devices: 14.8 us -> 0 us
  other arithmetic: 10.9 us -> 0 us
  local copies, waits for them, and re-layouts: 1.92 us -> 10.1 us
  matrix products: 7.91 us -> 0 us
    psum x1 -> x0, waiting for transfers between devices: 114 us -> none  [outer_sync(): total = lax.psum(decoded.reshape(rows, width), 'rep')]
    pallas_call x0 -> x1, Pallas kernels: none -> 80 us  [shards(): pl.pallas_call(kernel, out_shape=out_shape, in_specs=[any_spec] * 8, out_...]
    all_gather x1 -> x0, waiting for transfers between devices: 33.2 us -> none  [inner_backward(): piece = lax.all_gather(cotangent[0], 'fsdp', axis=0, tiled=True)]
    all_to_all x1 -> x0, starting transfers between devices: 14.7 us -> none  [inner_backward(): lax.all_to_all(normed, 'fsdp', split_axis=1, concat_axis=0, tiled=True)]
    unnamed x15 -> x20, local copies, waits for them, and re-layouts: 1.61 us -> 10.1 us
    dot_general x2 -> x0, matrix products: 7.91 us -> none  [the longest x1 5.89 us: inner_backward(): lax.dot_general(piece, weight_half, (((1,), (1,)), ((), ())), preferred_e...]
    convert_element_type x1 -> x0, other arithmetic: 3.8 us -> none  [inner_backward(): (values * lax.rsqrt(jnp.mean(values * values, axis=-1, keepdims=True) + 1...]
    mul x2 -> x0, other arithmetic: 2.33 us -> none  [outer_sync(): codes[0].astype(jnp.float32).reshape(rows, blocks, width // blocks)]
  transfers between devices with their start and end apart: 3 -> 0, of which waited for: 2 -> 0; matrix products, arithmetic and copies ran while one was open for 4% -> 0% of each run, Pallas kernels for 0% -> 0%
where the time goes in v1:
time: 91.1 us; the launch traced here: 90.8 us
  Pallas kernels  80 us (88%)
  local copies, waits for them, and re-layouts  10.1 us (11%)
    pallas_call x1, Pallas kernels, shards(): pl.pallas_call(kernel, out_shape=out_shape, in_specs=[any_spec] * 8, out_...  80 us
    unnamed x20, local copies, waits for them, and re-layouts  10.1 us

profile of v1, /device:TPU:1, one launch (start us, length us, event | category | flops | bytes accessed | tf_op | source)
XLA Modules:
  0.0 90.8 jit_solution(6929422527783056694)
XLA Ops:
  0.6 0.0 copy-start
  0.6 1.6 %copy-done = bf16[1,128,8192]{2,1,0:T(8,128)(2,1)S(1)} copy-done((bf16[1,128,8192]{2,1,0:T(8,128)(2,1)S(1)}, bf16[1,128,8192]{2,1,0:T(8,128)(2,1)}, u32[]{:S(2)}) %copy-start) | copy-done | bytes 2097176
  2.2 0.0 copy-start.1
  2.2 0.9 %copy-done.1 = f32[128,512]{1,0:T(8,128)S(1)} copy-done((f32[128,512]{1,0:T(8,128)S(1)}, f32[128,512]{1,0:T(8,128)}, u32[]{:S(2)}) %copy-start.1) | copy-done | bytes 262168
  3.2 0.0 copy-start.2
  3.2 0.9 %copy-done.2 = f32[128,512]{1,0:T(8,128)S(1)} copy-done((f32[128,512]{1,0:T(8,128)S(1)}, f32[128,512]{1,0:T(8,128)}, u32[]{:S(2)}) %copy-start.2) | copy-done | bytes 262168
  4.1 0.0 copy-start.3
  4.1 0.9 copy-done.3
  5.0 0.0 copy-start.4
  5.0 0.9 copy-done.4
  5.9 0.0 copy-start.5
  5.9 0.9 copy-done.5
  6.8 0.0 copy-start.6
  6.8 0.7 copy-done.6
  7.5 0.0 copy-start.7
  7.5 0.7 copy-done.7
  8.2 80.0 %sync_and_step.1 = (f32[1,128,512]{2,1,0:T(8,128)S(1)}, f32[1,128]{1,0:T(1,128)S(1)}, f32[128,512]{1,0:T(8,128)S(1)}, f32[128,512]{1,0:T(8,128)S(1)}) custom-call(bf16[1,128,8192]{2,1,0:T(8,128)(2,1)S(1)} %copy-done, bf16[1,128,512]{2,1,0:T(8,128)(2,1)S(1)} %copy-done.3, bf16[1,128,512]{2,1,0:T(8,128)(2,1)S(1)} %copy-done.4, f32[1,128]{1,0:T(1,128)S(1)} %copy-done.7, ...), custom_call_target="tpu_custom_call" | custom-call | tf_op jit(solution)/shard_map/sync_and_step/pallas_call | solution.py:256
  88.2 0.7 copy.16
  88.9 0.5 copy.17
  89.4 0.7 copy.18
  90.1 0.7 copy.19
Async XLA Ops:
  0.6 1.6 %copy-start = (bf16[1,128,8192]{2,1,0:T(8,128)(2,1)S(1)}, bf16[1,128,8192]{2,1,0:T(8,128)(2,1)}, u32[]{:S(2)}) copy-start(bf16[1,128,8192]{2,1,0:T(8,128)(2,1)} %act_hbm.1) | copy-start | bytes 6291460
  2.2 0.9 %copy-start.1 = (f32[128,512]{1,0:T(8,128)S(1)}, f32[128,512]{1,0:T(8,128)}, u32[]{:S(2)}) copy-start(f32[128,512]{1,0:T(8,128)} %global_hbm.1) | copy-start | bytes 786436
  3.2 0.9 %copy-start.2 = (f32[128,512]{1,0:T(8,128)S(1)}, f32[128,512]{1,0:T(8,128)}, u32[]{:S(2)}) copy-start(f32[128,512]{1,0:T(8,128)} %momentum_hbm.1) | copy-start | bytes 786436
  4.1 0.9 copy-start.3
  5.0 0.9 copy-start.4
  5.9 0.9 copy-start.5
  6.8 0.7 copy-start.6
  7.5 0.7 copy-start.7

commit v2 on v1

v2 whole, which is shorter than its diff:
```python
import functools
import math

import jax
import jax.numpy as jnp
from jax import lax
from jax.experimental import pallas as pl
from jax.experimental.pallas import tpu as pltpu
from jax.sharding import PartitionSpec as P

MESH = pl.DeviceIdType.MESH
YS, ZS, XS = 8, 4, 4
F32, BF16 = jnp.float32, jnp.bfloat16


def flip(value, mask):
    low, high = lax.rem(value, 2), value // 2
    if mask & 1:
        low = 1 - low
    if mask & 2:
        high = 1 - high
    return high * 2 + low


def column(row, eye):
    return jnp.sum(jnp.where(eye, row, 0.0), axis=1, keepdims=True)


def product(lhs, rhs):
    return lax.dot_general(lhs, rhs, (((0,), (0,)), ((), ())), preferred_element_type=F32)


def kernel(
    act_hbm, cot_hbm, codes_hbm, exps_hbm, summed_hbm, total_hbm,
    act, cot, normed_y, normed_z, recv_y, recv_z, cots_y, cots_z, codes, exps,
    part, from_z, up_half, down_half, ups, downs, decoded, x_in, x_sum, h_in, total,
    in_sem, out_sem, cy_s, cy_r, cz_s, cz_r, ay_s, ay_r, az_s, az_r, own_s,
    z_s, z_r, up_s, up_r, down_s, down_r, x1_s, x1_r, h_s, h_r, x2_s, x2_r,
):
    rep, pos = lax.axis_index("rep"), lax.axis_index("fsdp")
    zh, x = rep // XS, lax.rem(rep, XS)
    y, z, core = pos // (2 * ZS), lax.rem(pos // 2, ZS), lax.rem(pos, 2)
    width = act.shape[1]

    def at(yy=None, zz=None, cc=None, xx=None, hh=None):
        yy = y if yy is None else yy
        zz = z if zz is None else zz
        cc = core if cc is None else cc
        xx = x if xx is None else xx
        hh = zh if hh is None else hh
        return (hh * XS + xx, (yy * ZS + zz) * 2 + cc)

    def y_off(d):
        return lax.rem(y + d, YS)

    def x_off(d):
        return at(xx=lax.rem(x + d, XS))

    def send(src, dst, ssem, rsem, device):
        return pltpu.make_async_remote_copy(
            src_ref=src, dst_ref=dst, send_sem=ssem, recv_sem=rsem, device_id=device, device_id_type=MESH
        )

    def greet(device):
        pl.semaphore_signal(barrier, inc=1, device_id=device, device_id_type=MESH)

    other = at(hh=1 - zh)

    loads = [
        pltpu.make_async_copy(cot_hbm.at[0], cot, in_sem.at[0]),
        pltpu.make_async_copy(codes_hbm.at[0], codes, in_sem.at[1]),
        pltpu.make_async_copy(exps_hbm, exps, in_sem.at[2]),
        pltpu.make_async_copy(act_hbm.at[0], act, in_sem.at[3]),
    ]
    for load in loads:
        load.start()

    barrier = pltpu.get_barrier_semaphore()
    for device in [at(cc=1 - core), other] + [x_off(d) for d in range(1, XS)]:
        greet(device)
    for q in (1, 2, 3):
        greet(at(zz=flip(z, q)))

    @pl.when(core == 0)
    def _():
        for d in range(1, YS):
            for c in range(2):
                greet(at(yy=y_off(d), cc=c))

    @pl.when(core == 1)
    def _():
        for q in (1, 2, 3):
            greet(at(zz=flip(z, q), cc=0))
        greet(at(yy=y_off(1)))
        greet(at(yy=y_off(7)))

    eye = lax.broadcasted_iota(jnp.int32, (128, 128), 0) == lax.broadcasted_iota(
        jnp.int32, (128, 128), 1
    )
    loads[1].wait()
    loads[2].wait()
    scales = jnp.exp2(exps[...].astype(F32))
    for b in range(4):
        cols = slice(b * 128, (b + 1) * 128)
        scale = column(scales[b : b + 1, :], eye)
        decoded[:, cols] = (codes[:, cols].astype(F32) * scale).astype(BF16)

    pl.semaphore_wait(barrier, 15 + jnp.where(core == 0, 3, 2))

    loads[0].wait()
    first = [
        send(cot, cots_y.at[1, core], cy_s.at[0], cy_r.at[0], at(yy=y_off(1), cc=0)),
        send(cot, cots_y.at[7, core], cy_s.at[4], cy_r.at[4], at(yy=y_off(7), cc=0)),
    ]
    for copy in first:
        copy.start()

    def first_right():
        return send(cot, cots_z.at[z, core], cz_s.at[0], cz_r.at[0], at(zz=z + 1, cc=1))

    def first_left():
        return send(cot, cots_z.at[z, core], cz_s.at[3], cz_r.at[3], at(zz=z - 1, cc=1))

    @pl.when(z < ZS - 1)
    def _():
        first_right().start()

    @pl.when(z > 0)
    def _():
        first_left().start()

    x_parts = []
    for d in range(1, XS):
        rows = pl.ds(pl.multiple_of(lax.rem(x + d, XS) * 32, 32), 32)
        x_parts.append(send(decoded.at[rows], x_in.at[d - 1], x1_s.at[d - 1], x1_r.at[d - 1], x_off(d)))
    for copy in x_parts:
        copy.start()

    def across_0():
        return send(cot, cots_z.at[z, 0], own_s.at[0], cz_r.at[6], at(cc=1))

    def across_1():
        return send(cot, cots_y.at[0, 1], own_s.at[0], cy_r.at[8], at(cc=0))

    @pl.when(core == 0)
    def _():
        across_0().start()
        cots_y[0, 0] = cot[...]

    @pl.when(core == 1)
    def _():
        across_1().start()
        cots_z[z, 1] = cot[...]

    loads[3].wait()

    @pl.loop(0, 8)
    def _(group):
        rows = pl.ds(pl.multiple_of(group * 16, 16), 16)
        squares = jnp.zeros((16, 256), F32)
        for b in range(32):
            values = act[rows, b * 256 : (b + 1) * 256].astype(F32)
            squares += values * values
        mean = jnp.sum(squares, axis=1, keepdims=True) / width
        scale = lax.rsqrt(mean + 1e-05)
        for b in range(32):
            values = act[rows, b * 256 : (b + 1) * 256].astype(F32)
            result = (values * scale).astype(BF16)
            normed_y[b, rows, :] = result[:, :128]
            normed_z[b // ZS + (b % ZS) * YS, rows, :] = result[:, 128:]

    def push_y(k):
        zz = flip(z, 3 - k)
        for d in (4, 3, 5, 2, 6, 1, 7):
            yy = y_off(d)
            send(
                normed_y.at[yy * ZS + zz], recv_y.at[k, 2 * d + core], ay_s.at[k], ay_r.at[k], at(yy=yy, cc=0)
            ).start()

        @pl.when(core == 0)
        def _():
            recv_y[k, 0] = normed_y[y * ZS + zz]

        @pl.when(core == 1)
        def _():
            own_y(k).start()

    def own_y(k):
        zz = flip(z, 3 - k)
        return send(normed_y.at[y * ZS + zz], recv_y.at[k, 1], own_s.at[1 + k], ay_r.at[k], at(cc=0))

    offsets = (4, 3, 5, 2, 6, 1, 7, 0)
    groups = ((0,), (1, 2), (3, 4), (5, 6), (7,))

    def push_z(g):
        for i in groups[g]:
            yy = y_off(offsets[i])
            for q in (3, 2, 1):
                zz = flip(z, q)
                send(
                    normed_z.at[zz * YS + yy], recv_z.at[i, z * 2 + core],
                    az_s.at[g], az_r.at[g], at(zz=zz, cc=1),
                ).start()

        @pl.when(core == 0)
        def _():
            for i in groups[g]:
                own_z(g, i).start()

        @pl.when(core == 1)
        def _():
            for i in groups[g]:
                recv_z[i, z * 2 + 1] = normed_z[z * YS + y_off(offsets[i])]

    def own_z(g, i):
        return send(
            normed_z.at[z * YS + y_off(offsets[i])], recv_z.at[i, z * 2],
            own_s.at[1 + i], az_r.at[g], at(cc=1),
        )

    def z_copy(k):
        return send(part.at[k], from_z.at[k], z_s.at[k], z_r.at[k], at(zz=flip(z, 3 - k)))

    def multiply_y(k):
        pltpu.make_async_copy(recv_y.at[k, 1:16], recv_y.at[k, 1:16], ay_r.at[k]).wait()
        part[k] = product(recv_y[k].reshape(2048, 128), cots_y[...].reshape(2048, 512))
        if k < 3:
            z_copy(k).start()

    def multiply_z(g):
        i, n = groups[g][0], len(groups[g])
        pltpu.make_async_copy(recv_z.at[i : i + n, 0:7], recv_z.at[i : i + n, 0:7], az_r.at[g]).wait()
        for i in groups[g]:
            part[i] = product(recv_z[i].reshape(1024, 128), cots_z[...].reshape(1024, 512))

    def up_copy(s):
        src = part.at[0, :, 0:256] if s == 0 else part.at[2 * s - 1]
        dst = up_half if s == 0 else ups.at[s - 1]
        return send(src, dst, up_s.at[s], up_r.at[s], at(yy=y_off(1)))

    def down_copy(s):
        src = part.at[0, :, 256:512] if s == 0 else part.at[2 * s]
        dst = down_half if s == 0 else downs.at[s - 1]
        return send(src, dst, down_s.at[s], down_r.at[s], at(yy=y_off(7)))

    def chain(s):
        if s > 0:
            up_copy(s - 1).wait_recv()
        if s == 1:
            part[1, :, 0:256] = part[1, :, 0:256] + up_half[...]
        elif s > 1:
            part[2 * s - 1] = part[2 * s - 1] + ups[s - 2]
        up_copy(s).start()
        if s > 0:
            down_copy(s - 1).wait_recv()
        if s == 1:
            part[2, :, 256:512] = part[2, :, 256:512] + down_half[...]
        elif s > 1:
            part[2 * s] = part[2 * s] + downs[s - 2]
        down_copy(s).start()

    def ring_up(i):
        if i < 3:
            return send(cots_y.at[i], cots_y.at[i + 1], cy_s.at[i], cy_r.at[i], at(yy=y_off(1)))
        return send(cots_y.at[3, 0], cots_y.at[4, 0], cy_s.at[3], cy_r.at[3], at(yy=y_off(1)))

    def ring_down(i):
        if i < 3:
            return send(cots_y.at[8 - i], cots_y.at[7 - i], cy_s.at[4 + i], cy_r.at[4 + i], at(yy=y_off(7)))
        return send(cots_y.at[5, 1], cots_y.at[4, 1], cy_s.at[7], cy_r.at[7], at(yy=y_off(7)))

    def ring_wait(i):
        if i == 0:
            pltpu.make_async_copy(cots_y.at[1], cots_y.at[1], cy_r.at[0]).wait()
            pltpu.make_async_copy(cots_y.at[7], cots_y.at[7], cy_r.at[4]).wait()
        else:
            ring_up(i).wait_recv()
            ring_down(i).wait_recv()

    def ring_go(i):
        ring_up(i).start()
        ring_down(i).start()

    def right(h):
        return send(cots_z.at[z - h], cots_z.at[z - h], cz_s.at[h], cz_r.at[h], at(zz=z + 1))

    def left(h):
        return send(cots_z.at[z + h], cots_z.at[z + h], cz_s.at[3 + h], cz_r.at[3 + h], at(zz=z - 1))

    def line_wait(h):
        @pl.when(z >= h)
        def _():
            pltpu.make_async_copy(cots_z.at[0], cots_z.at[0], cz_r.at[h - 1]).wait()

        @pl.when(z < ZS - h)
        def _():
            pltpu.make_async_copy(cots_z.at[0], cots_z.at[0], cz_r.at[2 + h]).wait()

        if h < 3:

            @pl.when((z >= h) & (z < ZS - 1))
            def _():
                right(h).start()

            @pl.when((z < ZS - h) & (z > 0))
            def _():
                left(h).start()

    mine = pl.ds(pl.multiple_of(x * 32, 32), 32)
    h_copy = send(x_sum, h_in, h_s.at[0], h_r.at[0], other)
    totals = [
        send(total.at[mine], total.at[mine], x2_s.at[d - 1], x2_r.at[d - 1], x_off(d))
        for d in range(1, XS)
    ]

    def spread_total():
        h_copy.wait_recv()
        total[mine, :] = x_sum[...] + h_in[...]
        for copy in totals:
            copy.start()

    total_copy = pltpu.make_async_copy(total, total_hbm, out_sem.at[0])

    def write_total():
        for copy in totals:
            copy.wait_recv()
        total_copy.start()

    push_z(0)
    push_y(0)
    for copy in x_parts:
        copy.wait_recv()
    x_sum[...] = (
        decoded[mine, :].astype(F32) + x_in[0].astype(F32) + x_in[1].astype(F32) + x_in[2].astype(F32)
    )
    h_copy.start()

    @pl.when(core == 0)
    def _():
        push_z(1)
        ring_wait(0)
        ring_go(1)
        push_z(2)
        ring_wait(1)
        ring_go(2)
        push_y(1)
        push_z(3)
        ring_wait(2)
        ring_go(3)
        push_z(4)
        push_y(2)
        push_y(3)
        spread_total()
        across_1().wait_recv()
        ring_wait(3)
        multiply_y(0)
        multiply_y(1)
        multiply_y(2)
        write_total()
        multiply_y(3)
        for k in range(3):
            z_copy(k).wait_recv()
        part[3] = part[3] + from_z[0] + from_z[1] + from_z[2]
        result = pltpu.make_async_copy(part.at[3], summed_hbm, out_sem.at[1])
        result.start()
        result.wait()

    @pl.when(core == 1)
    def _():
        line_wait(1)
        push_z(1)
        line_wait(2)
        push_y(1)
        push_z(2)
        push_z(3)
        line_wait(3)
        push_y(2)
        push_z(4)
        across_0().wait_recv()
        multiply_z(0)
        chain(0)
        push_y(3)
        multiply_z(1)
        chain(1)
        spread_total()
        multiply_z(2)
        chain(2)
        write_total()
        multiply_z(3)
        chain(3)
        multiply_z(4)
        up_copy(3).wait_recv()
        down_copy(3).wait_recv()
        part[7] = part[7] + ups[2] + downs[2]
        result = pltpu.make_async_copy(part.at[7], summed_hbm, out_sem.at[1])
        result.start()
        result.wait()

    total_copy.wait()
    for copy in first + x_parts + [h_copy] + totals:
        copy.wait_send()
    for k in range(4):
        pltpu.make_async_copy(normed_y.at[0:7], normed_y.at[0:7], ay_s.at[k]).wait()
    for g in range(5):
        n = 3 * len(groups[g])
        pltpu.make_async_copy(normed_z.at[0:n], normed_z.at[0:n], az_s.at[g]).wait()

    @pl.when(z < ZS - 1)
    def _():
        first_right().wait_send()

    @pl.when(z > 0)
    def _():
        first_left().wait_send()

    @pl.when(core == 0)
    def _():
        across_0().wait_send()
        for g in range(5):
            for i in groups[g]:
                own_z(g, i).wait_send()
        for i in range(1, 4):
            ring_up(i).wait_send()
            ring_down(i).wait_send()
        for k in range(3):
            z_copy(k).wait_send()

    @pl.when(core == 1)
    def _():
        across_1().wait_send()
        for k in range(4):
            own_y(k).wait_send()
        for h in (1, 2):

            @pl.when((z >= h) & (z < ZS - 1))
            def _():
                right(h).wait_send()

            @pl.when((z < ZS - h) & (z > 0))
            def _():
                left(h).wait_send()

        for s in range(4):
            up_copy(s).wait_send()
            down_copy(s).wait_send()


def finish(
    summed_hbm, total_hbm, weight_hbm, gain_hbm, global_hbm, momentum_hbm,
    local_out, gain_out, global_out, momentum_out,
    summed, total, weight, gain, outer, mom, local, gain_new, in_sem, out_sem,
):
    sources = (total_hbm, momentum_hbm, global_hbm, summed_hbm, weight_hbm.at[0], gain_hbm)
    loads = [
        pltpu.make_async_copy(src, dst, in_sem.at[i])
        for i, (src, dst) in enumerate(zip(sources, (total, mom, outer, summed, weight, gain)))
    ]
    for load in loads:
        load.start()
    for load in loads[:3]:
        load.wait()
    average = total[...] / 8.0
    mom[...] = 0.9 * mom[...] + average
    outer[...] = outer[...] - 0.7 * (average + 0.9 * mom[...])
    stores = [
        pltpu.make_async_copy(mom, momentum_out, out_sem.at[0]),
        pltpu.make_async_copy(outer, global_out, out_sem.at[1]),
    ]
    stores[0].start()
    stores[1].start()
    for load in loads[3:]:
        load.wait()
    eye = lax.broadcasted_iota(jnp.int32, (128, 128), 0) == lax.broadcasted_iota(
        jnp.int32, (128, 128), 1
    )
    root = math.sqrt(8192)
    held = weight[...].astype(F32)
    weight_grad = column(gain[...], eye) * summed[...] / root
    local[...] = 0.5 * (held - 0.2 * weight_grad) + 0.5 * outer[...]
    stores.append(pltpu.make_async_copy(local, local_out.at[0], out_sem.at[2]))
    stores[2].start()
    gain_grad = jnp.sum(held * summed[...], axis=1, keepdims=True) / root
    gain_row = jnp.sum(jnp.where(eye, gain_grad, 0.0), axis=0, keepdims=True)
    gain_new[...] = gain[...] - 0.005 * gain_row
    stores.append(pltpu.make_async_copy(gain_new, gain_out, out_sem.at[3]))
    stores[3].start()
    for store in stores:
        store.wait()


def shards(
    activations, cotangent, local_weight, norm_gain, global_weight, momentum, codes, exponents
):
    rows, width = global_weight.shape
    anywhere = pl.BlockSpec(memory_space=pl.ANY)
    sem = pltpu.SemaphoreType.DMA
    whole = jax.ShapeDtypeStruct((rows, width), F32)
    summed, total = pl.pallas_call(
        kernel,
        out_shape=(whole, whole),
        in_specs=[anywhere] * 4,
        out_specs=(anywhere,) * 2,
        scratch_shapes=[
            pltpu.VMEM((128, 8192), BF16),
            pltpu.VMEM((128, 512), BF16),
            pltpu.VMEM((32, 128, 128), BF16),
            pltpu.VMEM((32, 128, 128), BF16),
            pltpu.VMEM((4, 16, 128, 128), BF16),
            pltpu.VMEM((8, 8, 128, 128), BF16),
            pltpu.VMEM((8, 2, 128, 512), BF16),
            pltpu.VMEM((4, 2, 128, 512), BF16),
            pltpu.VMEM((128, 512), BF16),
            pltpu.VMEM((4, 128), jnp.int32),
            pltpu.VMEM((8, 128, 512), F32),
            pltpu.VMEM((3, 128, 512), F32),
            pltpu.VMEM((128, 256), F32),
            pltpu.VMEM((128, 256), F32),
            pltpu.VMEM((3, 128, 512), F32),
            pltpu.VMEM((3, 128, 512), F32),
            pltpu.VMEM((128, 512), BF16),
            pltpu.VMEM((3, 32, 512), BF16),
            pltpu.VMEM((32, 512), F32),
            pltpu.VMEM((32, 512), F32),
            pltpu.VMEM((128, 512), F32),
            sem((4,)),
            sem((2,)),
            sem((8,)),
            sem((9,)),
            sem((6,)),
            sem((7,)),
            sem((4,)),
            sem((4,)),
            sem((5,)),
            sem((5,)),
            sem((9,)),
            sem((3,)),
            sem((3,)),
            sem((4,)),
            sem((4,)),
            sem((4,)),
            sem((4,)),
            sem((3,)),
            sem((3,)),
            sem((1,)),
            sem((1,)),
            sem((3,)),
            sem((3,)),
        ],
        compiler_params=pltpu.CompilerParams(
            collective_id=0, has_side_effects=True, vmem_limit_bytes=60 << 20
        ),
        name="exchange",
    )(activations, cotangent, codes, jnp.transpose(exponents[0]))
    return pl.pallas_call(
        finish,
        out_shape=(
            jax.ShapeDtypeStruct((1, rows, width), F32),
            jax.ShapeDtypeStruct((1, rows), F32),
            whole,
            whole,
        ),
        in_specs=[anywhere] * 6,
        out_specs=(anywhere,) * 4,
        scratch_shapes=[
            pltpu.VMEM((128, 512), F32),
            pltpu.VMEM((128, 512), F32),
            pltpu.VMEM((128, 512), BF16),
            pltpu.VMEM((1, 128), F32),
            pltpu.VMEM((128, 512), F32),
            pltpu.VMEM((128, 512), F32),
            pltpu.VMEM((128, 512), F32),
            pltpu.VMEM((1, 128), F32),
            sem((6,)),
            sem((4,)),
        ],
        compiler_params=pltpu.CompilerParams(vmem_limit_bytes=60 << 20),
        name="finish",
    )(summed, total, local_weight, norm_gain, global_weight, momentum)


def solution(mesh):
    placed = (
        P("rep", "fsdp", None),
        P("rep", "fsdp", None),
        P("rep", "fsdp", None),
        P("rep", "fsdp"),
        P("fsdp", None),
        P("fsdp", None),
        P("rep", "fsdp", None),
        P("rep", "fsdp", None),
    )
    return jax.shard_map(
        shards,
        mesh=mesh,
        in_specs=placed,
        out_specs=(P("rep", "fsdp", None), P("rep", "fsdp"), P("fsdp", None), P("fsdp", None)),
        check_vma=False,
    )
```

time: 91.1 us -> 73.3 us (0.80)
  local copies, waits for them, and re-layouts: 10.1 us -> 0 us
  Pallas kernels: 80 us -> 72.5 us
    unnamed x20 -> x0, local copies, waits for them, and re-layouts: 10.1 us -> none
    pallas_call x1 -> x2, Pallas kernels: 80 us -> 72.5 us  [the longest x1 70.3 us: shards(): pl.pallas_call(kernel, out_shape=(whole, whole), in_specs=[anywhere] * 4,...]
where the time goes in v2:
time: 73.3 us; the launch traced here: 73.1 us
  Pallas kernels  72.5 us (99%)
    pallas_call x1, Pallas kernels, shards(): pl.pallas_call(kernel, out_shape=(whole, whole), in_specs=[anywhere] * 4,...  70.3 us
    pallas_call x1, Pallas kernels, shards(): pl.pallas_call(finish, out_shape=(jax.ShapeDtypeStruct((1, rows, width),...  2.17 us

profile of v2, /device:TPU:1, one launch (start us, length us, event | category | flops | bytes accessed | tf_op | source)
XLA Modules:
  0.0 73.1 jit_solution(9646597021053625390)
XLA Ops:
  0.6 70.3 %exchange.1 = (f32[128,512]{1,0:T(8,128)}, f32[128,512]{1,0:T(8,128)}) custom-call(bf16[1,128,8192]{2,1,0:T(8,128)(2,1)} %act_hbm.1, bf16[1,128,512]{2,1,0:T(8,128)(2,1)} %cot_hbm.1, bf16[1,128,512]{2,1,0:T(8,128)(2,1)} %codes_hbm.1, s32[4,128]{1,0:T(4,128)} %bitcast.3), custom_call_target="tpu_custom_call" | custom-call | tf_op jit(solution)/shard_map/exchange/pallas_call | solution.py:498
  71.0 2.2 %finish.1 = (f32[1,128,512]{2,1,0:T(8,128)}, f32[1,128]{1,0:T(1,128)}, f32[128,512]{1,0:T(8,128)}, f32[128,512]{1,0:T(8,128)}) custom-call(f32[128,512]{1,0:T(8,128)} %get-tuple-element.6.summed_hbm, f32[128,512]{1,0:T(8,128)} %get-tuple-element.7.total_hbm, bf16[1,128,512]{2,1,0:T(8,128)(2,1)} %weight_hbm.1, f32[1,128]{1,0:T(1,128)} %gain_hbm.1, ...), custom_call_target="tpu_custom_call" | custom-call | tf_op jit(solution)/shard_map/finish/pallas_call | solution.py:554

commit v3 on v2

--- a/solution.py
+++ b/solution.py
@@ -33,9 +33,9 @@
 def kernel(
     act_hbm, cot_hbm, codes_hbm, exps_hbm, summed_hbm, total_hbm,
     act, cot, normed_y, normed_z, recv_y, recv_z, cots_y, cots_z, codes, exps,
-    part, from_z, up_half, down_half, ups, downs, decoded, x_in, x_sum, h_in, total,
+    part, from_z, ups, downs, decoded, x_in, x_sum, h_in, total,
     in_sem, out_sem, cy_s, cy_r, cz_s, cz_r, ay_s, ay_r, az_s, az_r, own_s,
-    z_s, z_r, up_s, up_r, down_s, down_r, x1_s, x1_r, h_s, h_r, x2_s, x2_r,
+    z_s, z_r, up_s, up_r, down_s, down_r, x1_s, x1_r, h_s, h_r, x2_s, x2_r, met,
 ):
     rep, pos = lax.axis_index("rep"), lax.axis_index("fsdp")
     zh, x = rep // XS, lax.rem(rep, XS)
@@ -76,8 +76,13 @@
         load.start()
 
     barrier = pltpu.get_barrier_semaphore()
-    for device in [at(cc=1 - core), other] + [x_off(d) for d in range(1, XS)]:
+    for device in [at(cc=1 - core)] + [x_off(d) for d in range(1, XS)]:
         greet(device)
+
+    @pl.when(zh == 0)
+    def _():
+        greet(other)
+
     for q in (1, 2, 3):
         greet(at(zz=flip(z, q)))
 
@@ -105,7 +110,11 @@
         scale = column(scales[b : b + 1, :], eye)
         decoded[:, cols] = (codes[:, cols].astype(F32) * scale).astype(BF16)
 
-    pl.semaphore_wait(barrier, 15 + jnp.where(core == 0, 3, 2))
+    pl.semaphore_wait(barrier, 14 + zh + jnp.where(core == 0, 3, 2))
+
+    @pl.when(zh == 1)
+    def _():
+        pl.semaphore_signal(met, inc=1, device_id=other, device_id_type=MESH)
 
     loads[0].wait()
     first = [
@@ -169,8 +178,17 @@
             normed_y[b, rows, :] = result[:, :128]
             normed_z[b // ZS + (b % ZS) * YS, rows, :] = result[:, 128:]
 
+    def goal(k):
+        if k == 0:
+            return jnp.where(z < 2, 3, 0)
+        if k == 1:
+            return lax.rem(12 - 2 * z, 5)
+        if k == 2:
+            return 1 + lax.rem(z, 2)
+        return z
+
     def push_y(k):
-        zz = flip(z, 3 - k)
+        zz = goal(k)
         for d in (4, 3, 5, 2, 6, 1, 7):
             yy = y_off(d)
             send(
@@ -186,8 +204,11 @@
             own_y(k).start()
 
     def own_y(k):
-        zz = flip(z, 3 - k)
+        zz = goal(k)
         return send(normed_y.at[y * ZS + zz], recv_y.at[k, 1], own_s.at[1 + k], ay_r.at[k], at(cc=0))
+
+    def sent_y(k):
+        pltpu.make_async_copy(normed_y.at[0:7], normed_y.at[0:7], ay_s.at[k]).wait()
 
     offsets = (4, 3, 5, 2, 6, 1, 7, 0)
     groups = ((0,), (1, 2), (3, 4), (5, 6), (7,))
@@ -212,6 +233,10 @@
             for i in groups[g]:
                 recv_z[i, z * 2 + 1] = normed_z[z * YS + y_off(offsets[i])]
 
+    def sent_z(g):
+        n = 3 * len(groups[g])
+        pltpu.make_async_copy(normed_z.at[0:n], normed_z.at[0:n], az_s.at[g]).wait()
+
     def own_z(g, i):
         return send(
             normed_z.at[z * YS + y_off(offsets[i])], recv_z.at[i, z * 2],
@@ -219,13 +244,27 @@
         )
 
     def z_copy(k):
-        return send(part.at[k], from_z.at[k], z_s.at[k], z_r.at[k], at(zz=flip(z, 3 - k)))
+        right = goal(k) > z
+        slot = goal(k) + jnp.where(right, 0, 4)
+        device = at(zz=z + jnp.where(right, 1, -1))
+        return send(part.at[k], from_z.at[slot], z_s.at[k], z_r.at[slot], device)
+
+    def inbox(slot):
+        pltpu.make_async_copy(from_z.at[slot], from_z.at[slot], z_r.at[slot]).wait()
+        return from_z[slot]
 
     def multiply_y(k):
         pltpu.make_async_copy(recv_y.at[k, 1:16], recv_y.at[k, 1:16], ay_r.at[k]).wait()
         part[k] = product(recv_y[k].reshape(2048, 128), cots_y[...].reshape(2048, 512))
-        if k < 3:
-            z_copy(k).start()
+
+    def pass_y(k):
+        right = goal(k) > z
+
+        @pl.when((right & (z > 0)) | (jnp.logical_not(right) & (z < ZS - 1)))
+        def _():
+            part[k] = part[k] + inbox(goal(k) + jnp.where(right, 0, 4))
+
+        z_copy(k).start()
 
     def multiply_z(g):
         i, n = groups[g][0], len(groups[g])
@@ -233,31 +272,38 @@
         for i in groups[g]:
             part[i] = product(recv_z[i].reshape(1024, 128), cots_z[...].reshape(1024, 512))
 
-    def up_copy(s):
-        src = part.at[0, :, 0:256] if s == 0 else part.at[2 * s - 1]
-        dst = up_half if s == 0 else ups.at[s - 1]
-        return send(src, dst, up_s.at[s], up_r.at[s], at(yy=y_off(1)))
-
-    def down_copy(s):
-        src = part.at[0, :, 256:512] if s == 0 else part.at[2 * s]
-        dst = down_half if s == 0 else downs.at[s - 1]
-        return send(src, dst, down_s.at[s], down_r.at[s], at(yy=y_off(7)))
+    def up_copy(s, h):
+        cols = slice(256 * h, 256 * h + 256)
+        src = part.at[max(2 * s - 1, 0), :, cols]
+        return send(src, ups.at[s, :, cols], up_s.at[s, h], up_r.at[s, h], at(yy=y_off(1)))
+
+    def down_copy(s, h):
+        cols = slice(256 * h, 256 * h + 256)
+        src = part.at[2 * s, :, cols]
+        return send(src, downs.at[s, :, cols], down_s.at[s, h], down_r.at[s, h], at(yy=y_off(7)))
+
+    def add_up(s, h, i):
+        if s > 0 or h == 0:
+            cols = slice(256 * h, 256 * h + 256)
+            up_copy(s, h).wait_recv()
+            part[i, :, cols] = part[i, :, cols] + ups[s, :, cols]
+
+    def add_down(s, h, i):
+        if s > 0 or h == 1:
+            cols = slice(256 * h, 256 * h + 256)
+            down_copy(s, h).wait_recv()
+            part[i, :, cols] = part[i, :, cols] + downs[s, :, cols]
 
     def chain(s):
-        if s > 0:
-            up_copy(s - 1).wait_recv()
-        if s == 1:
-            part[1, :, 0:256] = part[1, :, 0:256] + up_half[...]
-        elif s > 1:
-            part[2 * s - 1] = part[2 * s - 1] + ups[s - 2]
-        up_copy(s).start()
-        if s > 0:
-            down_copy(s - 1).wait_recv()
-        if s == 1:
-            part[2, :, 256:512] = part[2, :, 256:512] + down_half[...]
-        elif s > 1:
-            part[2 * s] = part[2 * s] + downs[s - 2]
-        down_copy(s).start()
+        if s == 0:
+            up_copy(0, 0).start()
+            down_copy(0, 1).start()
+        else:
+            for h in range(2):
+                add_up(s - 1, h, 2 * s - 1)
+                up_copy(s, h).start()
+                add_down(s - 1, h, 2 * s)
+                down_copy(s, h).start()
 
     def ring_up(i):
         if i < 3:
@@ -313,6 +359,19 @@
         for d in range(1, XS)
     ]
 
+    def gather_x():
+        for copy in x_parts:
+            copy.wait_recv()
+        x_sum[...] = (
+            decoded[mine, :].astype(F32) + x_in[0].astype(F32) + x_in[1].astype(F32) + x_in[2].astype(F32)
+        )
+
+        @pl.when(zh == 0)
+        def _():
+            pl.semaphore_wait(met, 1)
+
+        h_copy.start()
+
     def spread_total():
         h_copy.wait_recv()
         total[mine, :] = x_sum[...] + h_in[...]
@@ -327,84 +386,101 @@
         total_copy.start()
 
     push_z(0)
-    push_y(0)
-    for copy in x_parts:
-        copy.wait_recv()
-    x_sum[...] = (
-        decoded[mine, :].astype(F32) + x_in[0].astype(F32) + x_in[1].astype(F32) + x_in[2].astype(F32)
-    )
-    h_copy.start()
 
     @pl.when(core == 0)
     def _():
-        push_z(1)
+        push_y(0)
         ring_wait(0)
         ring_go(1)
-        push_z(2)
+        sent_z(0)
+        push_z(1)
         ring_wait(1)
         ring_go(2)
         push_y(1)
-        push_z(3)
+        gather_x()
+        sent_z(1)
+        push_z(2)
         ring_wait(2)
         ring_go(3)
-        push_z(4)
         push_y(2)
-        push_y(3)
-        spread_total()
+        sent_z(2)
+        push_z(3)
         across_1().wait_recv()
         ring_wait(3)
         multiply_y(0)
+        pass_y(0)
+        sent_y(1)
+        push_y(3)
+        sent_z(3)
+        push_z(4)
         multiply_y(1)
+        pass_y(1)
+        spread_total()
         multiply_y(2)
+        pass_y(2)
         write_total()
         multiply_y(3)
-        for k in range(3):
-            z_copy(k).wait_recv()
-        part[3] = part[3] + from_z[0] + from_z[1] + from_z[2]
+        @pl.when(z > 0)
+        def _():
+            part[3] = part[3] + inbox(z)
+
+        @pl.when(z < ZS - 1)
+        def _():
+            part[3] = part[3] + inbox(z + 4)
+
         result = pltpu.make_async_copy(part.at[3], summed_hbm, out_sem.at[1])
         result.start()
         result.wait()
+        sent_y(0)
+        sent_y(2)
+        sent_y(3)
+        sent_z(4)
 
     @pl.when(core == 1)
     def _():
         line_wait(1)
+        push_y(0)
+        sent_z(0)
         push_z(1)
         line_wait(2)
         push_y(1)
+        gather_x()
+        sent_z(1)
         push_z(2)
-        push_z(3)
         line_wait(3)
-        push_y(2)
-        push_z(4)
         across_0().wait_recv()
         multiply_z(0)
         chain(0)
-        push_y(3)
+        push_y(2)
+        sent_z(2)
+        push_z(3)
         multiply_z(1)
         chain(1)
-        spread_total()
+        sent_z(3)
+        push_z(4)
+        push_y(3)
         multiply_z(2)
         chain(2)
-        write_total()
+        spread_total()
         multiply_z(3)
         chain(3)
+        write_total()
         multiply_z(4)
-        up_copy(3).wait_recv()
-        down_copy(3).wait_recv()
-        part[7] = part[7] + ups[2] + downs[2]
+        for h in range(2):
+            add_up(3, h, 7)
+            add_down(3, h, 7)
         result = pltpu.make_async_copy(part.at[7], summed_hbm, out_sem.at[1])
         result.start()
         result.wait()
+        sent_y(0)
+        sent_y(1)
+        sent_y(2)
+        sent_y(3)
+        sent_z(4)
 
     total_copy.wait()
     for copy in first + x_parts + [h_copy] + totals:
         copy.wait_send()
-    for k in range(4):
-        pltpu.make_async_copy(normed_y.at[0:7], normed_y.at[0:7], ay_s.at[k]).wait()
-    for g in range(5):
-        n = 3 * len(groups[g])
-        pltpu.make_async_copy(normed_z.at[0:n], normed_z.at[0:n], az_s.at[g]).wait()
-
     @pl.when(z < ZS - 1)
     def _():
         first_right().wait_send()
@@ -440,9 +516,12 @@
             def _():
                 left(h).wait_send()
 
-        for s in range(4):
-            up_copy(s).wait_send()
-            down_copy(s).wait_send()
+        up_copy(0, 0).wait_send()
+        down_copy(0, 1).wait_send()
+        for s in range(1, 4):
+            for h in range(2):
+                up_copy(s, h).wait_send()
+                down_copy(s, h).wait_send()
 
 
 def finish(
@@ -512,11 +591,9 @@
             pltpu.VMEM((128, 512), BF16),
             pltpu.VMEM((4, 128), jnp.int32),
             pltpu.VMEM((8, 128, 512), F32),
-            pltpu.VMEM((3, 128, 512), F32),
-            pltpu.VMEM((128, 256), F32),
-            pltpu.VMEM((128, 256), F32),
-            pltpu.VMEM((3, 128, 512), F32),
-            pltpu.VMEM((3, 128, 512), F32),
+            pltpu.VMEM((7, 128, 512), F32),
+            pltpu.VMEM((4, 128, 512), F32),
+            pltpu.VMEM((4, 128, 512), F32),
             pltpu.VMEM((128, 512), BF16),
             pltpu.VMEM((3, 32, 512), BF16),
             pltpu.VMEM((32, 512), F32),
@@ -534,17 +611,18 @@
             sem((5,)),
             sem((9,)),
             sem((3,)),
-            sem((3,)),
-            sem((4,)),
-            sem((4,)),
-            sem((4,)),
-            sem((4,)),
+            sem((7,)),
+            sem((4, 2)),
+            sem((4, 2)),
+            sem((4, 2)),
+            sem((4, 2)),
             sem((3,)),
             sem((3,)),
             sem((1,)),
             sem((1,)),
             sem((3,)),
             sem((3,)),
+            pltpu.SemaphoreType.REGULAR,
         ],
         compiler_params=pltpu.CompilerParams(
             collective_id=0, has_side_effects=True, vmem_limit_bytes=60 << 20

time: 73.3 us -> 61.8 us (0.84)
  Pallas kernels: 72.5 us -> 61 us
    pallas_call x1, Pallas kernels: 70.3 us -> 58.8 us  [shards(): pl.pallas_call(kernel, out_shape=(whole, whole), in_specs=[anywhere] * 4,...]
where the time goes in v3:
time: 61.8 us; the launch traced here: 61.6 us
  Pallas kernels  61 us (99%)
  between operations  0.64 us (1%)
    pallas_call x1, Pallas kernels, shards(): pl.pallas_call(kernel, out_shape=(whole, whole), in_specs=[anywhere] * 4,...  58.8 us
    pallas_call x1, Pallas kernels, shards(): pl.pallas_call(finish, out_shape=(jax.ShapeDtypeStruct((1, rows, width),...  2.17 us

profile of v3, /device:TPU:1, one launch (start us, length us, event | category | flops | bytes accessed | tf_op | source)
XLA Modules:
  0.0 61.6 jit_solution(9027095169750099763)
XLA Ops:
  0.6 58.8 %exchange.1 = (f32[128,512]{1,0:T(8,128)}, f32[128,512]{1,0:T(8,128)}) custom-call(bf16[1,128,8192]{2,1,0:T(8,128)(2,1)} %act_hbm.1, bf16[1,128,512]{2,1,0:T(8,128)(2,1)} %cot_hbm.1, bf16[1,128,512]{2,1,0:T(8,128)(2,1)} %codes_hbm.1, s32[4,128]{1,0:T(4,128)} %bitcast.3), custom_call_target="tpu_custom_call" | custom-call | tf_op jit(solution)/shard_map/exchange/pallas_call | solution.py:577
  59.4 2.2 %finish.1 = (f32[1,128,512]{2,1,0:T(8,128)}, f32[1,128]{1,0:T(1,128)}, f32[128,512]{1,0:T(8,128)}, f32[128,512]{1,0:T(8,128)}) custom-call(f32[128,512]{1,0:T(8,128)} %get-tuple-element.6.summed_hbm, f32[128,512]{1,0:T(8,128)} %get-tuple-element.7.total_hbm, bf16[1,128,512]{2,1,0:T(8,128)(2,1)} %weight_hbm.1, f32[1,128]{1,0:T(1,128)} %gain_hbm.1, ...), custom_call_target="tpu_custom_call" | custom-call | tf_op jit(solution)/shard_map/finish/pallas_call | solution.py:632

commit v4 on v3

--- a/solution.py
+++ b/solution.py
@@ -68,9 +68,10 @@
 
     loads = [
         pltpu.make_async_copy(cot_hbm.at[0], cot, in_sem.at[0]),
+        pltpu.make_async_copy(act_hbm.at[0, 0:64], act.at[0:64], in_sem.at[3]),
+        pltpu.make_async_copy(act_hbm.at[0, 64:128], act.at[64:128], in_sem.at[4]),
         pltpu.make_async_copy(codes_hbm.at[0], codes, in_sem.at[1]),
         pltpu.make_async_copy(exps_hbm, exps, in_sem.at[2]),
-        pltpu.make_async_copy(act_hbm.at[0], act, in_sem.at[3]),
     ]
     for load in loads:
         load.start()
@@ -98,17 +99,6 @@
             greet(at(zz=flip(z, q), cc=0))
         greet(at(yy=y_off(1)))
         greet(at(yy=y_off(7)))
-
-    eye = lax.broadcasted_iota(jnp.int32, (128, 128), 0) == lax.broadcasted_iota(
-        jnp.int32, (128, 128), 1
-    )
-    loads[1].wait()
-    loads[2].wait()
-    scales = jnp.exp2(exps[...].astype(F32))
-    for b in range(4):
-        cols = slice(b * 128, (b + 1) * 128)
-        scale = column(scales[b : b + 1, :], eye)
-        decoded[:, cols] = (codes[:, cols].astype(F32) * scale).astype(BF16)
 
     pl.semaphore_wait(barrier, 14 + zh + jnp.where(core == 0, 3, 2))
 
@@ -138,13 +128,6 @@
     def _():
         first_left().start()
 
-    x_parts = []
-    for d in range(1, XS):
-        rows = pl.ds(pl.multiple_of(lax.rem(x + d, XS) * 32, 32), 32)
-        x_parts.append(send(decoded.at[rows], x_in.at[d - 1], x1_s.at[d - 1], x1_r.at[d - 1], x_off(d)))
-    for copy in x_parts:
-        copy.start()
-
     def across_0():
         return send(cot, cots_z.at[z, 0], own_s.at[0], cz_r.at[6], at(cc=1))
 
@@ -161,10 +144,7 @@
         across_1().start()
         cots_z[z, 1] = cot[...]
 
-    loads[3].wait()
-
-    @pl.loop(0, 8)
-    def _(group):
+    def normalise(group):
         rows = pl.ds(pl.multiple_of(group * 16, 16), 16)
         squares = jnp.zeros((16, 256), F32)
         for b in range(32):
@@ -178,6 +158,11 @@
             normed_y[b, rows, :] = result[:, :128]
             normed_z[b // ZS + (b % ZS) * YS, rows, :] = result[:, 128:]
 
+    loads[1].wait()
+    pl.loop(0, 4)(normalise)
+    loads[2].wait()
+    pl.loop(4, 8)(normalise)
+
     def goal(k):
         if k == 0:
             return jnp.where(z < 2, 3, 0)
@@ -187,13 +172,16 @@
             return 1 + lax.rem(z, 2)
         return z
 
-    def push_y(k):
+    def push_y(k, steps=(4, 3, 5, 2, 6, 1, 7)):
         zz = goal(k)
-        for d in (4, 3, 5, 2, 6, 1, 7):
+        for d in steps:
             yy = y_off(d)
             send(
                 normed_y.at[yy * ZS + zz], recv_y.at[k, 2 * d + core], ay_s.at[k], ay_r.at[k], at(yy=yy, cc=0)
             ).start()
+
+        if 1 not in steps:
+            return
 
         @pl.when(core == 0)
         def _():
@@ -359,6 +347,25 @@
         for d in range(1, XS)
     ]
 
+    x_parts = []
+    for d in range(1, XS):
+        rows = pl.ds(pl.multiple_of(lax.rem(x + d, XS) * 32, 32), 32)
+        x_parts.append(send(decoded.at[rows], x_in.at[d - 1], x1_s.at[d - 1], x1_r.at[d - 1], x_off(d)))
+
+    def share_codes():
+        eye = lax.broadcasted_iota(jnp.int32, (128, 128), 0) == lax.broadcasted_iota(
+            jnp.int32, (128, 128), 1
+        )
+        loads[3].wait()
+        loads[4].wait()
+        scales = jnp.exp2(exps[...].astype(F32))
+        for b in range(4):
+            cols = slice(b * 128, (b + 1) * 128)
+            scale = column(scales[b : b + 1, :], eye)
+            decoded[:, cols] = (codes[:, cols].astype(F32) * scale).astype(BF16)
+        for copy in x_parts:
+            copy.start()
+
     def gather_x():
         for copy in x_parts:
             copy.wait_recv()
@@ -389,28 +396,32 @@
 
     @pl.when(core == 0)
     def _():
-        push_y(0)
+        push_y(0, (4, 3, 5))
         ring_wait(0)
         ring_go(1)
+        push_y(0, (2, 6, 1, 7))
+        share_codes()
         sent_z(0)
         push_z(1)
+        push_y(1, (4, 3, 5))
         ring_wait(1)
         ring_go(2)
-        push_y(1)
+        push_y(1, (2, 6, 1, 7))
         gather_x()
         sent_z(1)
         push_z(2)
+        push_y(2, (4, 3, 5))
         ring_wait(2)
         ring_go(3)
-        push_y(2)
+        push_y(2, (2, 6, 1, 7))
         sent_z(2)
         push_z(3)
+        push_y(3, (4, 3, 5))
         across_1().wait_recv()
         ring_wait(3)
         multiply_y(0)
+        push_y(3, (2, 6, 1, 7))
         pass_y(0)
-        sent_y(1)
-        push_y(3)
         sent_z(3)
         push_z(4)
         multiply_y(1)
@@ -432,6 +443,7 @@
         result.start()
         result.wait()
         sent_y(0)
+        sent_y(1)
         sent_y(2)
         sent_y(3)
         sent_z(4)
@@ -440,10 +452,12 @@
     def _():
         line_wait(1)
         push_y(0)
+        share_codes()
         sent_z(0)
         push_z(1)
+        push_y(1, (4, 3, 5))
         line_wait(2)
-        push_y(1)
+        push_y(1, (2, 6, 1, 7))
         gather_x()
         sent_z(1)
         push_z(2)
@@ -451,9 +465,9 @@
         across_0().wait_recv()
         multiply_z(0)
         chain(0)
-        push_y(2)
         sent_z(2)
         push_z(3)
+        push_y(2)
         multiply_z(1)
         chain(1)
         sent_z(3)
@@ -599,7 +613,7 @@
             pltpu.VMEM((32, 512), F32),
             pltpu.VMEM((32, 512), F32),
             pltpu.VMEM((128, 512), F32),
-            sem((4,)),
+            sem((5,)),
             sem((2,)),
             sem((8,)),
             sem((9,)),

time: 61.8 us -> 61 us (0.987)
  Pallas kernels: 61 us -> 59.6 us
    pallas_call x1, Pallas kernels: 58.8 us -> 57.5 us  [shards(): pl.pallas_call(kernel, out_shape=(whole, whole), in_specs=[anywhere] * 4,...]
where the time goes in v4:
time: 61 us; the launch traced here: 60.3 us
  Pallas kernels  59.6 us (98%)
  between operations  0.64 us (1%)
    pallas_call x1, Pallas kernels, shards(): pl.pallas_call(kernel, out_shape=(whole, whole), in_specs=[anywhere] * 4,...  57.5 us
    pallas_call x1, Pallas kernels, shards(): pl.pallas_call(finish, out_shape=(jax.ShapeDtypeStruct((1, rows, width),...  2.17 us

profile of v4, /device:TPU:1, one launch (start us, length us, event | category | flops | bytes accessed | tf_op | source)
XLA Modules:
  0.0 60.3 jit_solution(17207458356356246908)
XLA Ops:
  0.6 57.5 %exchange.1 = (f32[128,512]{1,0:T(8,128)}, f32[128,512]{1,0:T(8,128)}) custom-call(bf16[1,128,8192]{2,1,0:T(8,128)(2,1)} %act_hbm.1, bf16[1,128,512]{2,1,0:T(8,128)(2,1)} %cot_hbm.1, bf16[1,128,512]{2,1,0:T(8,128)(2,1)} %codes_hbm.1, s32[4,128]{1,0:T(4,128)} %bitcast.3), custom_call_target="tpu_custom_call" | custom-call | tf_op jit(solution)/shard_map/exchange/pallas_call | solution.py:591
  58.1 2.2 %finish.1 = (f32[1,128,512]{2,1,0:T(8,128)}, f32[1,128]{1,0:T(1,128)}, f32[128,512]{1,0:T(8,128)}, f32[128,512]{1,0:T(8,128)}) custom-call(f32[128,512]{1,0:T(8,128)} %get-tuple-element.6.summed_hbm, f32[128,512]{1,0:T(8,128)} %get-tuple-element.7.total_hbm, bf16[1,128,512]{2,1,0:T(8,128)(2,1)} %weight_hbm.1, f32[1,128]{1,0:T(1,128)} %gain_hbm.1, ...), custom_call_target="tpu_custom_call" | custom-call | tf_op jit(solution)/shard_map/finish/pallas_call | solution.py:646

commit v5 on v4

--- a/solution.py
+++ b/solution.py
@@ -480,12 +480,17 @@
         chain(3)
         write_total()
         multiply_z(4)
+        results = []
         for h in range(2):
             add_up(3, h, 7)
             add_down(3, h, 7)
-        result = pltpu.make_async_copy(part.at[7], summed_hbm, out_sem.at[1])
-        result.start()
-        result.wait()
+            cols = slice(256 * h, 256 * h + 256)
+            results.append(
+                pltpu.make_async_copy(part.at[7, :, cols], summed_hbm.at[:, cols], out_sem.at[1 + h])
+            )
+            results[h].start()
+        for result in results:
+            result.wait()
         sent_y(0)
         sent_y(1)
         sent_y(2)
@@ -614,7 +619,7 @@
             pltpu.VMEM((32, 512), F32),
             pltpu.VMEM((128, 512), F32),
             sem((5,)),
-            sem((2,)),
+            sem((3,)),
             sem((8,)),
             sem((9,)),
             sem((6,)),

time: 61 us -> 61 us (level)
  no operation moved by 1% of the time
where the time goes in v5:
time: 61 us; the launch traced here: 60.2 us
  Pallas kernels  59.6 us (98%)
  between operations  0.64 us (1%)
    pallas_call x1, Pallas kernels, shards(): pl.pallas_call(kernel, out_shape=(whole, whole), in_specs=[anywhere] * 4,...  57.4 us
    pallas_call x1, Pallas kernels, shards(): pl.pallas_call(finish, out_shape=(jax.ShapeDtypeStruct((1, rows, width),...  2.17 us

profile of v5, /device:TPU:1, one launch (start us, length us, event | category | flops | bytes accessed | tf_op | source)
XLA Modules:
  0.0 60.2 jit_solution(8785327274893038050)
XLA Ops:
  0.6 57.4 %exchange.1 = (f32[128,512]{1,0:T(8,128)}, f32[128,512]{1,0:T(8,128)}) custom-call(bf16[1,128,8192]{2,1,0:T(8,128)(2,1)} %act_hbm.1, bf16[1,128,512]{2,1,0:T(8,128)(2,1)} %cot_hbm.1, bf16[1,128,512]{2,1,0:T(8,128)(2,1)} %codes_hbm.1, s32[4,128]{1,0:T(4,128)} %bitcast.3), custom_call_target="tpu_custom_call" | custom-call | tf_op jit(solution)/shard_map/exchange/pallas_call | solution.py:596
  58.1 2.2 %finish.1 = (f32[1,128,512]{2,1,0:T(8,128)}, f32[1,128]{1,0:T(1,128)}, f32[128,512]{1,0:T(8,128)}, f32[128,512]{1,0:T(8,128)}) custom-call(f32[128,512]{1,0:T(8,128)} %get-tuple-element.6.summed_hbm, f32[128,512]{1,0:T(8,128)} %get-tuple-element.7.total_hbm, bf16[1,128,512]{2,1,0:T(8,128)(2,1)} %weight_hbm.1, f32[1,128]{1,0:T(1,128)} %gain_hbm.1, ...), custom_call_target="tpu_custom_call" | custom-call | tf_op jit(solution)/shard_map/finish/pallas_call | solution.py:651
